TPU v7x, 32 devices: a whole 2x2x4 slice. The times are simulated.
32 devices in a mesh: req: 8 (over z, x), mlp: 4 (over y, core).
Axes of the slice: x: 2, y: 2, z: 4, core: 2. Of those that a mesh axis runs over, the one named last changes fastest.
Arguments:
- tokens: bfloat16 [4096, 4096], P('req'), may hold values from -16 to 16
- grid_sides: int32 [16, 2], P('req'), may hold values from 10 to 14, as said below
- offsets: int32 [16], P('req'), may hold values from 0 to 201, as said below
- merge_rows: int32 [1024, 4], P('req'), may hold values from 0 to 401, as said below
- routes: int32 [1024, 1], replicated, may hold values from 0 to 7; in each aligned block of 128 rows (0 to 127, 128 to 255, ...) at most 16 rows name the same one
- norm_gain: float32 [2, 4096], replicated, may hold values from 0.5 to 1.5
- norm_bias: float32 [2, 4096], replicated, may hold values from -1.5 to 1.5
- layer_scale: float32 [2, 4096], replicated, may hold values from 0.2 to 1
- qkv_weight: bfloat16 [4096, 6144], P('req', 'mlp'), may hold values from -2.34375 to 2.34375
- out_weight: bfloat16 [2048, 4096], P('mlp', 'req'), may hold values from -0.125 to 0.125
- gate_up: bfloat16 [2, 4096, 4096], P(None, 'req', 'mlp'), may hold values from -0.09375 to 0.09375
- down_weight: bfloat16 [4096, 4096], P('mlp', 'req'), may hold values from -0.09375 to 0.09375
- merge_gain: float32 [4, 4096], P(None, 'mlp'), may hold values from 0.5 to 1.5
- merge_bias: float32 [4, 4096], P(None, 'mlp'), may hold values from -1.5 to 1.5
- merge_weight: bfloat16 [4, 4096, 2048], P(None, 'mlp', 'req'), may hold values from -0.1875 to 0.1875
Outputs:
- embeds: bfloat16 [1024, 2048], P('req', 'mlp')
- token_norms: float32 [1024], P('req')
- max_logits: float32 [16, 16], P('req', 'mlp')
Inputs may be any that keep to these rules, and one draw needn't show every extreme that they name: `grid_sides`: sides are even; the first 2 of all 16 images are 14 x 14 and the last image is 10 x 10. `offsets`: the images of a group are packed in order from in-group row 0: image g * 2 + j starts at the sum of 5 + h w over images g * 2 to g * 2 + j - 1. `merge_rows`: for slot k of group g, image i = g * 2 + k div 64 of grid h x w at offset o and m = k mod 64: if m < (h / 2)(w / 2), the entries are o + 5 + (2 a + e) w + 2 b + f for (e, f) = (0, 0), (0, 1), (1, 0), (1, 1), with a = m div (w / 2), b = m mod (w / 2); otherwise all four are 0. `routes`: among the 128 slots of one group, no value appears more than 16 times.
All inputs are finite; a program needn't handle non-finite values.
Results may differ from a plain program's by a relative error of at most 0.017.
Values may be sent and summed in bfloat16 or wider, within the bound.
A program may use at most 128 MiB of HBM per device.

v0:
```python
import math

import jax
import jax.numpy as jnp
from jax import lax
from jax.sharding import PartitionSpec as P

HEAD = 128
OUT = 2048
MSLOT = 64
CAP = 16


EPS = 1e-06


def layer_norm(values, scale_vec, shift_vec):
    center = jnp.mean(values, axis=-1, keepdims=True)
    offset_vals = values - center
    spread = jnp.mean(offset_vals * offset_vals, axis=-1, keepdims=True)
    return offset_vals * lax.rsqrt(spread + EPS) * scale_vec + shift_vec


def row_layout(grid_part, starts, row_count, head_size):
    position = jnp.arange(row_count, dtype=jnp.int32)
    lengths = 5 + grid_part[:, 0] * grid_part[:, 1]
    inside = (
        (position[:, None] >= starts[None, :]) & (position[:, None] < (starts + lengths)[None, :])
    ).astype(jnp.int32)
    present = jnp.sum(inside, axis=1)
    numbers = jnp.arange(grid_part.shape[0], dtype=jnp.int32)
    image_id = jnp.sum(inside * numbers[None, :], axis=1) + present - 1
    local_row = position - jnp.sum(inside * starts[None, :], axis=1)
    height = jnp.sum(inside * grid_part[None, :, 0], axis=1) + 1 - present
    breadth = jnp.sum(inside * grid_part[None, :, 1], axis=1) + 1 - present
    is_patch = (local_row >= 5) & (present > 0)
    patch_idx = jnp.maximum(local_row - 5, 0)
    coord_y = jnp.where(
        is_patch,
        (2.0 * (patch_idx // breadth).astype(jnp.float32) + 1.0) / height.astype(jnp.float32) - 1.0,
        0.0,
    )
    coord_x = jnp.where(
        is_patch,
        (2.0 * (patch_idx % breadth).astype(jnp.float32) + 1.0) / breadth.astype(jnp.float32) - 1.0,
        0.0,
    )
    quarter = head_size // 4
    frequency = math.pi * 100.0 ** (-jnp.arange(quarter, dtype=jnp.float32) / quarter)
    angle_y = (coord_y[:, None] * frequency[None, :])[:, None, :]
    angle_x = (coord_x[:, None] * frequency[None, :])[:, None, :]
    return (image_id, (jnp.cos(angle_y), jnp.sin(angle_y), jnp.cos(angle_x), jnp.sin(angle_x)))


def rotate(vectors, tables):
    cos_y, sin_y, cos_x, sin_x = tables
    quarter = vectors.shape[-1] // 4
    upper_y = vectors[..., :quarter]
    lower_y = vectors[..., quarter : 2 * quarter]
    upper_x = vectors[..., 2 * quarter : 3 * quarter]
    lower_x = vectors[..., 3 * quarter :]
    return jnp.concatenate(
        [
            upper_y * cos_y - lower_y * sin_y,
            upper_y * sin_y + lower_y * cos_y,
            upper_x * cos_x - lower_x * sin_x,
            upper_x * sin_x + lower_x * cos_x,
        ],
        axis=-1,
    )


def attend(queries, key_rows, values, image_id, numbers):
    scores = jnp.einsum(
        "qhd,khd->hqk", queries, key_rows, preferred_element_type=jnp.float32
    ) / math.sqrt(queries.shape[-1])
    same_image = image_id[:, None] == image_id[None, :]
    scores = jnp.where(same_image[None], scores, -jnp.inf)
    row_peak = jnp.max(scores, axis=-1)
    expo_vals = jnp.exp(scores - row_peak[..., None])
    weights = (expo_vals / jnp.sum(expo_vals, axis=-1, keepdims=True)).astype(jnp.bfloat16)
    attended = jnp.einsum(
        "hqk,khd->qhd", weights, values, preferred_element_type=jnp.float32
    ).astype(jnp.bfloat16)
    owned = image_id[None, None, :] == numbers[:, None, None]
    logits = jnp.max(jnp.where(owned, row_peak[None], -jnp.inf), axis=-1)
    return (attended, logits)


def on_device(
    tokens,
    grid_sides,
    offsets,
    merge_rows,
    routes,
    norm_gain,
    norm_bias,
    layer_scale,
    qkv_weight,
    out_weight,
    gate_up,
    down_weight,
    merge_gain,
    merge_bias,
    merge_weight,
):
    row_count = tokens.shape[0]
    model_width = tokens.shape[1]
    groups = lax.axis_size("req")
    shards = lax.axis_size("mlp")
    group_id = lax.axis_index("req")
    member = lax.axis_index("mlp")
    piece_width = model_width // shards
    start_col = member * piece_width
    slot_count = merge_rows.shape[0]
    numbers = jnp.arange(grid_sides.shape[0], dtype=jnp.int32)
    image_id, tables = row_layout(grid_sides, offsets, row_count, HEAD)
    normed = layer_norm(tokens.astype(jnp.float32), norm_gain[0], norm_bias[0]).astype(jnp.bfloat16)
    columns = normed
    mixed_qkv = jnp.dot(
        columns,
        lax.all_gather(qkv_weight, "req", axis=0, tiled=True),
        preferred_element_type=jnp.float32,
    )
    heads_here = qkv_weight.shape[1] // (3 * HEAD)
    mixed_qkv = mixed_qkv.reshape(row_count, heads_here, 3, HEAD)
    queries = rotate(mixed_qkv[:, :, 0], tables).astype(jnp.bfloat16)
    key_rows = rotate(mixed_qkv[:, :, 1], tables).astype(jnp.bfloat16)
    values = mixed_qkv[:, :, 2].astype(jnp.bfloat16)
    attended, logits = attend(queries, key_rows, values, image_id, numbers)
    attended_flat = attended.reshape(row_count, heads_here * HEAD)
    head_terms = jnp.dot(
        attended_flat,
        lax.all_gather(out_weight, "req", axis=1, tiled=True),
        preferred_element_type=jnp.float32,
    )
    attn_sum = lax.psum(head_terms.astype(jnp.bfloat16), "mlp").astype(jnp.float32)
    residual = (tokens.astype(jnp.float32) + layer_scale[0] * attn_sum).astype(jnp.bfloat16)
    resid_piece = lax.dynamic_slice_in_dim(residual, start_col, piece_width, 1)
    normed_two = layer_norm(residual.astype(jnp.float32), norm_gain[1], norm_bias[1]).astype(
        jnp.bfloat16
    )
    columns = normed_two
    gate_pair = jnp.einsum(
        "rk,pkn->prn",
        columns,
        lax.all_gather(gate_up, "req", axis=1, tiled=True),
        preferred_element_type=jnp.float32,
    )
    hidden = (jax.nn.silu(gate_pair[0]) * gate_pair[1]).astype(jnp.bfloat16)
    hidden_terms = jnp.dot(
        hidden,
        lax.all_gather(down_weight, "req", axis=1, tiled=True),
        preferred_element_type=jnp.float32,
    )
    ffn_piece = lax.psum_scatter(
        hidden_terms.astype(jnp.bfloat16), "mlp", scatter_dimension=1, tiled=True
    ).astype(jnp.float32)
    own_scale_two = lax.dynamic_slice_in_dim(layer_scale[1], start_col, piece_width, 0)
    final_piece = (resid_piece.astype(jnp.float32) + own_scale_two * ffn_piece).astype(jnp.bfloat16)
    merged = final_piece[merge_rows].astype(jnp.float32)
    totals, squares = lax.psum(
        (jnp.sum(merged, axis=(1, 2)), jnp.sum(merged * merged, axis=(1, 2))), "mlp"
    )
    center = totals / (4 * model_width)
    spread = squares / (4 * model_width) - center * center
    scaled = (
        (merged - center[:, None, None]) * lax.rsqrt(spread + EPS)[:, None, None] * merge_gain[None]
        + merge_bias[None]
    ).astype(jnp.bfloat16)
    scaled_flat = scaled.reshape(slot_count, 4 * piece_width)
    piece_rows = lax.all_gather(merge_weight, "req", axis=2, tiled=True)
    merge_terms = jnp.dot(
        scaled_flat,
        piece_rows.reshape(4 * piece_width, piece_rows.shape[2]),
        preferred_element_type=jnp.float32,
    )
    projected = lax.psum_scatter(
        merge_terms.astype(jnp.bfloat16), "mlp", scatter_dimension=1, tiled=True
    ).astype(jnp.float32)
    slot_ids = jnp.arange(slot_count, dtype=jnp.int32)
    owner_grid = grid_sides[slot_ids // MSLOT]
    is_live = slot_ids % MSLOT < owner_grid[:, 0] // 2 * (owner_grid[:, 1] // 2)
    projected = jnp.where(is_live[:, None], projected, 0.0).astype(jnp.bfloat16)
    out_cols = projected.shape[1]
    own_routes = lax.dynamic_slice_in_dim(routes, group_id * slot_count, slot_count, 0)[:, 0]
    onehot = (own_routes[:, None] == jnp.arange(groups, dtype=jnp.int32)[None, :]).astype(jnp.int32)
    before = jnp.cumsum(onehot, axis=0) - onehot
    ranks = jnp.sum(before * onehot, axis=1)
    send_rows = (
        jnp.zeros((groups * CAP, out_cols), jnp.bfloat16)
        .at[own_routes * CAP + ranks]
        .set(projected)
    )
    received = lax.all_to_all(
        send_rows.reshape(groups, CAP, out_cols), "req", split_axis=0, concat_axis=0, tiled=True
    )
    embeds = received.reshape(groups * CAP, out_cols)
    row_squares = jnp.sum(jnp.square(embeds.astype(jnp.float32)), axis=1)
    total_squares = lax.psum(row_squares, "mlp")
    token_norms = jnp.sqrt(total_squares / OUT + EPS)
    return (embeds, token_norms, logits)


def solution(mesh):
    placed = (
        P("req", None),
        P("req", None),
        P("req"),
        P("req", None),
        P(),
        P(),
        P(),
        P(),
        P("req", "mlp"),
        P("mlp", "req"),
        P(None, "req", "mlp"),
        P("mlp", "req"),
        P(None, "mlp"),
        P(None, "mlp"),
        P(None, "mlp", "req"),
    )
    return jax.shard_map(
        on_device,
        mesh=mesh,
        in_specs=placed,
        out_specs=(P("req", "mlp"), P("req"), P("req", "mlp")),
        check_vma=False,
    )
```

profile of v0, /device:TPU:0, one launch (start us, length us, event | category | flops | bytes accessed | tf_op | source)
XLA Modules:
  0.0 1053.9 jit_solution(7051907031724275753)
XLA Ops:
  7.2 0.7 all-gather.6.cloned.1.call-update
  8.0 0.7 all-gather.8.cloned.1.call-update
  8.7 1.1 slice_reduce_fusion
  9.8 0.9 add_add_fusion.1
  10.7 0.8 select_reduce_fusion.5
  11.5 2.8 convert_reduce_fusion
  14.3 1.2 fusion.4
  15.6 0.1 add_select_fusion.7
  15.7 0.2 broadcast_compare_fusion
  15.9 3.0 multiply_cosine_fusion.1
  19.0 170.4 %all-gather.6.cloned.1.call-done = bf16[4096,1536]{1,0:T(8,128)(2,1)} async-done(((bf16[512,1536]{1,0:T(8,128)(2,1)}), bf16[4096,1536]{1,0:T(8,128)(2,1)}) %all-gather.6.cloned.1.call-update) | async-done | bytes 12582928 | tf_op jit(solution)/shard_map/all_gather | solution.py:122
  189.4 11.7 %fusion.16 = f32[512,1536]{0,1:T(8,128)S(1)} fusion(bf16[4096,1536]{1,0:T(8,128)(2,1)} %all-gather.6.cloned.1.call-done, bf16[512,4096]{1,0:T(8,128)(2,1)} %param.15, f32[4096]{0:T(1024)S(1)} %bitcast.60, f32[4096]{0:T(1024)S(1)} %bitcast.59, f32[512]{0:T(512)S(1)} %add_rsqrt_fusion.1, f32[512]{0:T(512)S(1)} %broadcast_multiply_fusion.1), kind=kOutput, calls=%fused_computation.25 | convolution fusion | flops 6455033856 | bytes 19959808 | tf_op jit(solution)/shard_map/dot_general | solution.py:120
  201.0 0.2 fusion.98
  201.2 1.5 copy-done.8
  202.7 0.3 copy.46
  203.0 0.3 copy.47
  203.4 2.2 subtract_convert_fusion.3
  205.6 0.9 subtract_convert_fusion.1
  206.5 2.1 fusion.26
  208.6 0.9 fusion.27
  209.5 2.7 fusion.39
  212.2 52.4 %all-gather.8.cloned.1.call-done = bf16[512,4096]{1,0:T(8,128)(2,1)} async-done(((bf16[512,512]{1,0:T(8,128)(2,1)}), bf16[512,4096]{1,0:T(8,128)(2,1)}) %all-gather.8.cloned.1.call-update) | async-done | bytes 4194320 | tf_op jit(solution)/shard_map/all_gather | solution.py:134
  264.6 6.5 convolution_convert_fusion.1
  271.2 0.5 all-gather.10.cloned.1.call-update
  271.8 0.5 all-gather.12.cloned.1.call-update
  272.4 0.3 reduce-scatter.3.cloned.1.call-start
  272.7 82.3 %all-reduce.3.cloned.1.call-done = bf16[512,4096]{1,0:T(8,128)(2,1)} async-done(((bf16[512,4096]{1,0:T(8,128)(2,1)}), bf16[512,4096]{1,0:T(8,128)(2,1)}) %all-reduce.3.cloned.1.call-update) | async-done | bytes 4194320 | tf_op jit(solution)/shard_map/psum | solution.py:137
  355.0 5.6 convert_reduce_fusion.1
  360.6 1.9 copy-done.3
  362.5 1.2 fusion.8
  363.7 221.3 %all-gather.10.cloned.1.call-done = bf16[2,4096,1024]{2,1,0:T(8,128)(2,1)} async-done(((bf16[2,512,1024]{2,1,0:T(8,128)(2,1)}), bf16[2,4096,1024]{2,1,0:T(8,128)(2,1)}) %all-gather.10.cloned.1.call-update) | async-done | bytes 16777232 | tf_op jit(solution)/shard_map/all_gather | solution.py:147
  585.1 15.0 %fusion.29 = f32[2,512,1024]{2,1,0:T(8,128)} fusion(bf16[2,4096,1024]{2,1,0:T(8,128)(2,1)} %all-gather.10.cloned.1.call-done, bf16[512,4096]{1,0:T(8,128)(2,1)} %copy-done.3, f32[4096]{0:T(1024)S(1)} %bitcast.58, f32[4096]{0:T(1024)S(1)} %bitcast.57, f32[512]{0:T(512)S(1)} %add_rsqrt_fusion, f32[512]{0:T(512)S(1)} %broadcast_multiply_fusion), kind=kOutput, calls=%fused_computation.41 | convolution fusion | flops 8602517504 | bytes 25202688 | tf_op jit(solution)/shard_map/rk,pkn->prn/dot_general | solution.py:144
  600.1 110.7 %all-gather.12.cloned.1.call-done = bf16[1024,4096]{1,0:T(8,128)(2,1)} async-done(((bf16[1024,512]{1,0:T(8,128)(2,1)}), bf16[1024,4096]{1,0:T(8,128)(2,1)}) %all-gather.12.cloned.1.call-update) | async-done | bytes 8388624 | tf_op jit(solution)/shard_map/all_gather | solution.py:153
  710.8 11.2 %convolution_convert_fusion = bf16[512,4096]{1,0:T(8,128)(2,1)} fusion(bf16[1024,4096]{1,0:T(8,128)(2,1)} %all-gather.12.cloned.1.call-done, f32[2,512,1024]{2,1,0:T(8,128)} %fusion.29), kind=kOutput, calls=%fused_computation.21 | convolution fusion | flops 4300210176 | bytes 16777216 | tf_op jit(solution)/shard_map/dot_general | solution.py:151
  722.0 0.7 all-gather.14.cloned.1.call-update
  722.7 0.3 reduce-scatter.5.cloned.1.call-start
  723.0 0.1 copy.41
  723.3 41.5 %reduce-scatter.3.cloned.1.call-done = bf16[512,1024]{1,0:T(8,128)(2,1)} async-done(((bf16[512,4096]{1,0:T(8,128)(2,1)}), bf16[512,1024]{1,0:T(8,128)(2,1)}) %reduce-scatter.3.cloned.1.call-update) | async-done | bytes 1048592 | tf_op jit(solution)/shard_map/reduce_scatter | solution.py:156
  764.8 2.0 add_convert_fusion
  766.8 2.1 gather_fusion.1
  768.8 0.7 reshape.383
  769.6 0.2 convert_reduce_fusion.2
  769.8 0.1 reshape.384
  769.9 0.1 reduce_sum.142
  770.0 1.0 multiply_reduce_fusion
  771.0 5.7 all-reduce
  776.8 217.8 %all-gather.14.cloned.1.call-done = bf16[4,1024,2048]{2,1,0:T(8,128)(2,1)} async-done(((bf16[4,1024,256]{2,1,0:T(8,128)(2,1)}), bf16[4,1024,2048]{2,1,0:T(8,128)(2,1)}) %all-gather.14.cloned.1.call-update) | async-done | bytes 16777232 | tf_op jit(solution)/shard_map/all_gather | solution.py:172
  994.6 10.1 fusion.28
  1004.9 0.2 reduce_window_sum.11
  1005.1 0.2 select_reduce_fusion
  1005.3 0.1 copy.35
  1005.4 0.1 copy.45
  1005.5 0.1 fusion.73
  1005.7 0.6 gather_fusion
  1006.3 0.1 fusion.72
  1006.4 0.2 fusion.82
  1006.6 18.2 %reduce-scatter.5.cloned.1.call-done = bf16[128,512]{1,0:T(8,128)(2,1)} async-done(((bf16[128,2048]{1,0:T(8,128)(2,1)}), bf16[128,512]{1,0:T(8,128)(2,1)}) %reduce-scatter.5.cloned.1.call-update) | async-done | bytes 131088 | tf_op jit(solution)/shard_map/reduce_scatter | solution.py:178
  1024.8 2.1 scatter_custom_fusion
  1026.9 5.5 all-to-all-start
  1032.4 0.7 select_reduce_fusion.1
  1033.1 6.7 all-to-all-done
  1040.0 5.9 psum.31
  1045.9 0.5 add_sqrt_fusion
  1046.4 0.7 copy.66
  (58 shorter events, 0.9 us)
Async XLA Ops:
  7.2 997.6 %copy-start = (s32[1024,1]{0,1:T(1,128)S(1)}, s32[1024,1]{0,1:T(1,128)}, u32[]{:S(2)}) copy-start(s32[1024,1]{0,1:T(1,128)} %param.19) | copy-start | bytes 12292
  7.2 182.2 %all-gather.6.cloned.1.call-start = ((), (), s32[]{:S(2)}) async-start(), calls=%async_computation.3 | async-start | bytes 14155776 | tf_op jit(solution)/shard_map/all_gather | solution.py:122
  7.9 256.7 %all-gather.8.cloned.1.call-start = ((), (), s32[]{:S(2)}) async-start(), calls=%async_computation.4 | async-start | bytes 4718592 | tf_op jit(solution)/shard_map/all_gather | solution.py:134
  8.7 346.4 %all-reduce.3.cloned.1.call-start = ((), (), s32[]{:S(2)}) async-start(), calls=%async_computation.5 | async-start | bytes 8388608 | tf_op jit(solution)/shard_map/psum | solution.py:137
  8.7 5.6 copy-start.2
  11.4 7.5 copy-start.11
  11.4 7.5 copy-start.12
  201.0 1.7 copy-start.8
  203.4 2.2 copy-start.4
  203.4 2.2 copy-start.5
  203.4 2.2 copy-start.6
  203.4 2.2 copy-start.7
  271.2 1.5 copy-start.13
  271.2 313.9 %all-gather.10.cloned.1.call-start = ((), (), s32[]{:S(2)}) async-start(), calls=%async_computation.6 | async-start | bytes 18874368 | tf_op jit(solution)/shard_map/all_gather | solution.py:147
  271.8 439.0 %all-gather.12.cloned.1.call-start = ((), (), s32[]{:S(2)}) async-start(), calls=%async_computation.7 | async-start | bytes 9437184 | tf_op jit(solution)/shard_map/all_gather | solution.py:153
  272.4 492.4 %reduce-scatter.3.cloned.1.call-start = ((), (), s32[]{:S(2)}) async-start(), calls=%async_computation.8 | async-start | bytes 5242880 | tf_op jit(solution)/shard_map/reduce_scatter | solution.py:156
  360.6 1.9 copy-start.3
  721.9 1.1 copy-start.14
  721.9 272.7 %all-gather.14.cloned.1.call-start = ((), (), s32[]{:S(2)}) async-start(), calls=%async_computation.9 | async-start | bytes 18874368 | tf_op jit(solution)/shard_map/all_gather | solution.py:172
  722.7 302.1 %reduce-scatter.5.cloned.1.call-start = ((), (), s32[]{:S(2)}) async-start(), calls=%async_computation.10 | async-start | bytes 655360 | tf_op jit(solution)/shard_map/reduce_scatter | solution.py:178
  768.8 225.8 %copy-start.9 = (f32[4,1024]{1,0:T(4,128)S(1)}, f32[4,1024]{1,0:T(4,128)}, u32[]{:S(2)}) copy-start(f32[4,1024]{1,0:T(4,128)} %param.28) | copy-start | bytes 49156
  768.8 225.8 %copy-start.10 = (f32[4,1024]{1,0:T(4,128)S(1)}, f32[4,1024]{1,0:T(4,128)}, u32[]{:S(2)}) copy-start(f32[4,1024]{1,0:T(4,128)} %param.27) | copy-start | bytes 49156
  994.6 11.0 %copy-start.1 = (s32[2,2]{1,0:T(2,128)S(1)}, s32[2,2]{1,0:T(2,128)}, u32[]{:S(2)}) copy-start(s32[2,2]{1,0:T(2,128)} %param.16) | copy-start | bytes 52
  1026.9 12.9 %all-to-all-start = ((bf16[8,16,512]{2,1,0:T(8,128)(2,1)}), bf16[8,16,512]{2,1,0:T(8,128)(2,1)S(1)}, u32[]{:S(2)}, u32[]{:S(2)}) async-start(bf16[8,16,512]{2,1,0:T(8,128)(2,1)} %bitcast.18), calls=%async_computation.2 | async-start | bytes 262144 | tf_op jit(solution)/shard_map/all_to_all | solution.py:195
Sparse Core Ops, SparseCore 0:
  10.2 179.1 all-gather.5
  191.4 73.1 all-gather.7
  271.3 83.6 all-reduce.2
  357.3 227.7 all-gather.9
  587.1 123.5 all-gather.11
  722.1 42.6 reduce-scatter.2
  766.8 227.7 all-gather.13
  1004.9 19.8 reduce-scatter.4
where the time goes:
time: 1050 us
  waiting for transfers between devices  925 us (88%)
  matrix products  59.2 us (6%)
  other arithmetic  27.4 us (3%)
  between operations  14.5 us (1%)
  blocking collectives  11.6 us (1%)
    all_gather x1, waiting for transfers between devices, on_device(): lax.all_gather(gate_up, 'req', axis=1, tiled=True)  221 us
    all_gather x1, waiting for transfers between devices, on_device(): piece_rows = lax.all_gather(merge_weight, 'req', axis=2, tiled=True)  218 us
    all_gather x1, waiting for transfers between devices, on_device(): lax.all_gather(qkv_weight, 'req', axis=0, tiled=True)  170 us
    all_gather x1, waiting for transfers between devices, on_device(): lax.all_gather(down_weight, 'req', axis=1, tiled=True)  111 us
    psum x1, waiting for transfers between devices, on_device(): lax.psum(head_terms.astype(jnp.bfloat16), 'mlp').astype(jnp.float32)  82.3 us
    all_gather x1, waiting for transfers between devices, on_device(): lax.all_gather(out_weight, 'req', axis=1, tiled=True)  52.4 us
    reduce_scatter x1, waiting for transfers between devices, on_device(): lax.psum_scatter(hidden_terms.astype(jnp.bfloat16), 'mlp', scatter_dimens...  41.5 us
  transfers between devices with their start and end apart: 9, of which 9 were waited for; matrix products, arithmetic and copies ran while one was open for 6% of the time, Pallas kernels for 0%

commit v1 on v0

--- a/solution.py
+++ b/solution.py
@@ -1,14 +1,20 @@
+import functools
 import math
 
 import jax
 import jax.numpy as jnp
 from jax import lax
+from jax.experimental import pallas as pl
+from jax.experimental.pallas import tpu as pltpu
 from jax.sharding import PartitionSpec as P
+
+MESH = pl.DeviceIdType.MESH
 
 HEAD = 128
 OUT = 2048
 MSLOT = 64
 CAP = 16
+GMAX = 14
 
 
 EPS = 1e-06
@@ -87,6 +93,112 @@
     return (attended, logits)
 
 
+def ring_place(index, n):
+    side = index % 2
+    return (1 - side) * (index // 2) + side * (n - 1 - index // 2)
+
+
+def ring_device(place, n):
+    wrapped = (place + 2 * n) % n
+    late = wrapped // (n // 2)
+    return (1 - late) * (2 * wrapped) + late * (2 * (n - 1 - wrapped) + 1)
+
+
+def region(ref, kind, owner, size, first, count):
+    if kind == "col":
+        return ref.at[pl.ds(first, count), pl.ds(pl.multiple_of(owner * size, 128), size)]
+    rows = pl.ds(pl.multiple_of(owner * size + first, 16), count)
+    return ref.at[rows, :] if kind == "row" else ref.at[:, rows, :]
+
+
+def own_rows(ref, kind, first, count):
+    return ref.at[:, pl.ds(first, count), :] if kind == "mid" else ref.at[pl.ds(first, count), :]
+
+
+def ring_kernel(n, plan, units, extra, *refs):
+    count = len(plan)
+    ins = refs[:count]
+    outs = refs[count + extra : 2 * count + extra]
+    send_sem, recv_sem, local_sem = refs[2 * count + extra :]
+    me = lax.axis_index("req")
+    place = ring_place(me, n)
+    right, left = ring_device(place + 1, n), ring_device(place - 1, n)
+    barrier = pltpu.get_barrier_semaphore()
+    for neighbour in (left, right):
+        pl.semaphore_signal(barrier, inc=1, device_id={"req": neighbour}, device_id_type=MESH)
+    pl.semaphore_wait(barrier, 2)
+    steps = n // 2
+    started = {}
+    for step in range(steps):
+        for u, (i, first, rows) in enumerate(units):
+            kind, size = plan[i]
+            for way in (0, 1):
+                if step > 0:
+                    started[u, way, step - 1].wait_recv()
+                sign = 1 if way == 0 else -1
+                owner = ring_device(place - sign * step, n)
+                begin, length = first, rows
+                if step == steps - 1:
+                    upper = (rows // 2 + 15) // 16 * 16
+                    begin, length = (first, upper) if way == 0 else (first + upper, rows - upper)
+                target = region(outs[i], kind, owner, size, begin, length)
+                copy = pltpu.make_async_remote_copy(
+                    src_ref=own_rows(ins[i], kind, begin, length) if step == 0 else target,
+                    dst_ref=target,
+                    send_sem=send_sem.at[u, way, step],
+                    recv_sem=recv_sem.at[u, way, step],
+                    device_id={"req": right if way == 0 else left},
+                    device_id_type=MESH,
+                )
+                copy.start()
+                started[u, way, step] = copy
+        if step == 0:
+            local = []
+            for i, (kind, size) in enumerate(plan):
+                total = ins[i].shape[-2]
+                keep = pltpu.make_async_copy(
+                    own_rows(ins[i], kind, 0, total),
+                    region(outs[i], kind, me, size, 0, total),
+                    local_sem.at[i],
+                )
+                keep.start()
+                local.append(keep)
+    for (u, way, step), copy in started.items():
+        if step == steps - 1:
+            copy.wait_recv()
+        copy.wait_send()
+    for keep in local:
+        keep.wait()
+
+
+def ring_gather(arrays, kinds, cuts, collective_id, after=()):
+    n = lax.axis_size("req")
+    plan, units, shapes, moved = [], [], [], 0
+    for i, (array, kind, cut) in enumerate(zip(arrays, kinds, cuts)):
+        axis = array.ndim - 1 if kind == "col" else array.ndim - 2
+        shape = list(array.shape)
+        plan.append((kind, shape[axis]))
+        shape[axis] *= n
+        shapes.append(jax.ShapeDtypeStruct(tuple(shape), array.dtype))
+        rows = array.shape[-2] // cut
+        units += [(i, c * rows, rows) for c in range(cut)]
+        moved += math.prod(shape) * 2
+    return pl.pallas_call(
+        functools.partial(ring_kernel, n, tuple(plan), tuple(units), len(after)),
+        out_shape=shapes,
+        in_specs=[pl.BlockSpec(memory_space=pl.ANY)] * (len(arrays) + len(after)),
+        out_specs=[pl.BlockSpec(memory_space=pl.ANY)] * len(arrays),
+        scratch_shapes=[
+            pltpu.SemaphoreType.DMA((len(units), 2, n // 2)),
+            pltpu.SemaphoreType.DMA((len(units), 2, n // 2)),
+            pltpu.SemaphoreType.DMA((len(arrays),)),
+        ],
+        compiler_params=pltpu.CompilerParams(collective_id=collective_id, has_side_effects=True),
+        cost_estimate=pl.CostEstimate(flops=0, bytes_accessed=moved * 12, transcendentals=0),
+        name="ring_gather",
+    )(*arrays, *after)
+
+
 def on_device(
     tokens,
     grid_sides,
@@ -104,11 +216,12 @@
     merge_bias,
     merge_weight,
 ):
-    row_count = tokens.shape[0]
+    images = grid_sides.shape[0]
+    row_count = min(tokens.shape[0], -(-images * (5 + GMAX * GMAX) // 16) * 16)
+    tokens = tokens[:row_count]
     model_width = tokens.shape[1]
     groups = lax.axis_size("req")
     shards = lax.axis_size("mlp")
-    group_id = lax.axis_index("req")
     member = lax.axis_index("mlp")
     piece_width = model_width // shards
     start_col = member * piece_width
@@ -117,9 +230,10 @@
     image_id, tables = row_layout(grid_sides, offsets, row_count, HEAD)
     normed = layer_norm(tokens.astype(jnp.float32), norm_gain[0], norm_bias[0]).astype(jnp.bfloat16)
     columns = normed
+    qkv_all, out_all = ring_gather([qkv_weight, out_weight], ["row", "col"], [2, 1], 0)
     mixed_qkv = jnp.dot(
         columns,
-        lax.all_gather(qkv_weight, "req", axis=0, tiled=True),
+        qkv_all,
         preferred_element_type=jnp.float32,
     )
     heads_here = qkv_weight.shape[1] // (3 * HEAD)
@@ -131,10 +245,13 @@
     attended_flat = attended.reshape(row_count, heads_here * HEAD)
     head_terms = jnp.dot(
         attended_flat,
-        lax.all_gather(out_weight, "req", axis=1, tiled=True),
-        preferred_element_type=jnp.float32,
-    )
-    attn_sum = lax.psum(head_terms.astype(jnp.bfloat16), "mlp").astype(jnp.float32)
+        out_all,
+        preferred_element_type=jnp.float32,
+    ).astype(jnp.bfloat16)
+    gate_all, down_all = ring_gather(
+        [gate_up, down_weight], ["mid", "col"], [2, 2], 1, after=(head_terms[:16, :128],)
+    )
+    attn_sum = lax.psum(head_terms, "mlp").astype(jnp.float32)
     residual = (tokens.astype(jnp.float32) + layer_scale[0] * attn_sum).astype(jnp.bfloat16)
     resid_piece = lax.dynamic_slice_in_dim(residual, start_col, piece_width, 1)
     normed_two = layer_norm(residual.astype(jnp.float32), norm_gain[1], norm_bias[1]).astype(
@@ -144,13 +261,13 @@
     gate_pair = jnp.einsum(
         "rk,pkn->prn",
         columns,
-        lax.all_gather(gate_up, "req", axis=1, tiled=True),
+        gate_all,
         preferred_element_type=jnp.float32,
     )
     hidden = (jax.nn.silu(gate_pair[0]) * gate_pair[1]).astype(jnp.bfloat16)
     hidden_terms = jnp.dot(
         hidden,
-        lax.all_gather(down_weight, "req", axis=1, tiled=True),
+        down_all,
         preferred_element_type=jnp.float32,
     )
     ffn_piece = lax.psum_scatter(
@@ -158,7 +275,9 @@
     ).astype(jnp.float32)
     own_scale_two = lax.dynamic_slice_in_dim(layer_scale[1], start_col, piece_width, 0)
     final_piece = (resid_piece.astype(jnp.float32) + own_scale_two * ffn_piece).astype(jnp.bfloat16)
-    merged = final_piece[merge_rows].astype(jnp.float32)
+    live = -(-(GMAX // 2) ** 2 // 8) * 8
+    picked = merge_rows.reshape(images, MSLOT, 4)[:, :live].reshape(images * live, 4)
+    merged = final_piece[picked].astype(jnp.float32)
     totals, squares = lax.psum(
         (jnp.sum(merged, axis=(1, 2)), jnp.sum(merged * merged, axis=(1, 2))), "mlp"
     )
@@ -167,35 +286,41 @@
     scaled = (
         (merged - center[:, None, None]) * lax.rsqrt(spread + EPS)[:, None, None] * merge_gain[None]
         + merge_bias[None]
+    )
+    sent = images * live
+    is_live = (
+        jnp.arange(live, dtype=jnp.int32)[None, :]
+        < (grid_sides[:, 0] // 2 * (grid_sides[:, 1] // 2))[:, None]
+    ).reshape(sent)
+    scaled = jnp.where(is_live[:, None, None], scaled, 0.0).astype(jnp.bfloat16)
+    (scaled_all,) = ring_gather([scaled.reshape(sent, 4 * piece_width)], ["row"], [1], 2)
+    merge_terms = jnp.dot(
+        scaled_all,
+        merge_weight.reshape(4 * piece_width, merge_weight.shape[2]),
+        preferred_element_type=jnp.float32,
     ).astype(jnp.bfloat16)
-    scaled_flat = scaled.reshape(slot_count, 4 * piece_width)
-    piece_rows = lax.all_gather(merge_weight, "req", axis=2, tiled=True)
-    merge_terms = jnp.dot(
-        scaled_flat,
-        piece_rows.reshape(4 * piece_width, piece_rows.shape[2]),
-        preferred_element_type=jnp.float32,
-    )
-    projected = lax.psum_scatter(
-        merge_terms.astype(jnp.bfloat16), "mlp", scatter_dimension=1, tiled=True
-    ).astype(jnp.float32)
-    slot_ids = jnp.arange(slot_count, dtype=jnp.int32)
-    owner_grid = grid_sides[slot_ids // MSLOT]
-    is_live = slot_ids % MSLOT < owner_grid[:, 0] // 2 * (owner_grid[:, 1] // 2)
-    projected = jnp.where(is_live[:, None], projected, 0.0).astype(jnp.bfloat16)
-    out_cols = projected.shape[1]
-    own_routes = lax.dynamic_slice_in_dim(routes, group_id * slot_count, slot_count, 0)[:, 0]
-    onehot = (own_routes[:, None] == jnp.arange(groups, dtype=jnp.int32)[None, :]).astype(jnp.int32)
-    before = jnp.cumsum(onehot, axis=0) - onehot
-    ranks = jnp.sum(before * onehot, axis=1)
-    send_rows = (
-        jnp.zeros((groups * CAP, out_cols), jnp.bfloat16)
-        .at[own_routes * CAP + ranks]
-        .set(projected)
+    targets = routes[:, 0].reshape(groups, slot_count)
+    earlier = jnp.arange(slot_count)[None, :] < jnp.arange(slot_count)[:, None]
+    same = (targets[:, :, None] == targets[:, None, :]) & earlier[None]
+    ranks = jnp.sum(same.astype(jnp.int32), axis=2)
+    rows_out = groups * CAP
+    dest = targets * rows_out + jnp.arange(groups, dtype=jnp.int32)[:, None] * CAP + ranks
+    dest = dest.reshape(groups, images, MSLOT)[:, :, :live].reshape(groups * sent)
+    chosen = (jnp.arange(groups * rows_out, dtype=jnp.int32)[:, None] == dest[None, :]).astype(
+        jnp.bfloat16
+    )
+    placed_rows = jnp.dot(chosen, merge_terms, preferred_element_type=jnp.float32).astype(
+        jnp.bfloat16
     )
     received = lax.all_to_all(
-        send_rows.reshape(groups, CAP, out_cols), "req", split_axis=0, concat_axis=0, tiled=True
-    )
-    embeds = received.reshape(groups * CAP, out_cols)
+        placed_rows.reshape(groups, rows_out, merge_terms.shape[1]),
+        "req",
+        split_axis=0,
+        concat_axis=0,
+        tiled=True,
+    )
+    partial = received.transpose(1, 0, 2).reshape(rows_out, groups * merge_terms.shape[1])
+    embeds = lax.psum_scatter(partial, "mlp", scatter_dimension=1, tiled=True)
     row_squares = jnp.sum(jnp.square(embeds.astype(jnp.float32)), axis=1)
     total_squares = lax.psum(row_squares, "mlp")
     token_norms = jnp.sqrt(total_squares / OUT + EPS)

time: 1050 us -> 668 us (0.64)
  waiting for transfers between devices: 925 us -> 57 us
  Pallas kernels: 0 us -> 479 us
  matrix products: 59.2 us -> 44 us
  blocking collectives: 11.6 us -> 26.5 us
    all_gather x5 -> x0, waiting for transfers between devices: 773 us -> none  [the longest x1 221 us: on_device(): lax.all_gather(gate_up, 'req', axis=1, tiled=True)]
    pallas_call x0 -> x3, Pallas kernels: none -> 479 us  [ring_gather(): pl.pallas_call(functools.partial(ring_kernel, n, tuple(plan), tuple(units...]
    psum x1, waiting for transfers between devices: 82.3 us -> 0.02 us  [on_device(): attn_sum = lax.psum(head_terms, 'mlp').astype(jnp.float32)]
    dot_general x5, matrix products: 54.5 us -> 39.1 us  [the longest x1 12.2 us: on_device(): jnp.einsum('rk,pkn->prn', columns, gate_all, preferred_element_type=jnp.f...]
    all_to_all x0 -> x1, blocking collectives: none -> 14.7 us  [on_device(): lax.all_to_all(placed_rows.reshape(groups, rows_out, merge_terms.shape[1]...]
  transfers between devices with their start and end apart: 9 -> 3, of which waited for: 9 -> 2; matrix products, arithmetic and copies ran while one was open for 6% -> 0% of each run, Pallas kernels for 0% -> 36%
where the time goes in v1:
time: 668 us; the launch traced here: 667 us
  Pallas kernels  479 us (72%)
  waiting for transfers between devices  57 us (9%)
  matrix products  44 us (7%)
  other arithmetic  29.3 us (4%)
  blocking collectives  26.5 us (4%)
  local copies, waits for them, and re-layouts  16.8 us (3%)
  between operations  14.1 us (2%)
    pallas_call x3, Pallas kernels, ring_gather(): pl.pallas_call(functools.partial(ring_kernel, n, tuple(plan), tuple(units...  479 us
    reduce_scatter x1, waiting for transfers between devices, on_device(): lax.psum_scatter(hidden_terms.astype(jnp.bfloat16), 'mlp', scatter_dimens...  36.9 us
    reduce_scatter x1, waiting for transfers between devices, on_device(): embeds = lax.psum_scatter(partial, 'mlp', scatter_dimension=1, tiled=True)  19.3 us
    all_to_all x1, blocking collectives, on_device(): lax.all_to_all(placed_rows.reshape(groups, rows_out, merge_terms.shape[1]...  14.7 us
  transfers between devices with their start and end apart: 3, of which 2 were waited for; matrix products, arithmetic and copies ran while one was open for 0% of the time, Pallas kernels for 36%

profile of v1, /device:TPU:0, one launch (start us, length us, event | category | flops | bytes accessed | tf_op | source)
XLA Modules:
  0.0 666.9 jit_solution(13958182120560161319)
XLA Ops:
  7.2 1.0 fusion.78
  8.2 0.9 fusion.79
  9.0 2.5 convert_reduce_fusion
  11.5 3.0 fusion.4
  14.5 163.2 %ring_gather.3 = (bf16[4096,1536]{1,0:T(8,128)(2,1)}, bf16[512,4096]{1,0:T(8,128)(2,1)}) custom-call(bf16[512,1536]{1,0:T(8,128)(2,1)} %refs_0_.2, bf16[512,512]{1,0:T(8,128)(2,1)} %refs_1_.2), custom_call_target="tpu_custom_call" | custom-call | bytes 201326592 | tf_op jit(solution)/shard_map/ring_gather/pallas_call | solution.py:186
  177.7 11.2 %fusion.17 = f32[416,1536]{0,1:T(8,128)S(1)} fusion(bf16[4096,1536]{1,0:T(8,128)(2,1)} %get-tuple-element.7, f32[4096]{0:T(1024)S(1)} %bitcast.78, f32[4096]{0:T(1024)S(1)} %bitcast.77, f32[416]{0:T(512)S(1)} %add_rsqrt_fusion.1, f32[416]{0:T(512)S(1)} %broadcast_multiply_fusion.1, bf16[512,4096]{1,0:T(8,128)(2,1)} %param.15), kind=kOutput, calls=%fused_computation.25 | convolution fusion | flops 5244715008 | bytes 18582784 | tf_op jit(solution)/shard_map/dot_general | solution.py:234
  188.9 1.2 fusion.76
  190.1 0.9 slice.109
  191.0 0.2 multiply_reduce_fusion.3
  191.3 0.1 select_reduce_fusion.4
  191.4 1.3 copy.42
  192.6 1.5 copy.43
  194.2 0.1 add_select_fusion.3
  194.3 1.5 multiply_cosine_fusion.1
  195.9 4.1 subtract_convert_fusion.3
  200.0 1.9 subtract_convert_fusion.1
  201.9 0.2 broadcast_compare_fusion
  202.1 0.3 copy.41
  202.4 3.6 fusion.27
  206.0 0.8 fusion.28
  206.8 1.3 fusion.39
  208.1 0.9 copy-done.10
  209.0 3.8 convolution_convert_fusion
  212.8 1.3 slice.120.refs_2_
  214.1 0.7 all-reduce.3.cloned.1.call-update
  214.8 0.3 reduce-scatter.3.cloned.1.call-start
  215.1 239.6 %ring_gather.4 = (bf16[2,4096,1024]{2,1,0:T(8,128)(2,1)}, bf16[1024,4096]{1,0:T(8,128)(2,1)}) custom-call(bf16[2,512,1024]{2,1,0:T(8,128)(2,1)} %refs_0_.3, bf16[1024,512]{1,0:T(8,128)(2,1)} %refs_1_.3, bf16[16,128]{1,0:T(8,128)(2,1)} %slice.120.refs_2_), custom_call_target="tpu_custom_call" | custom-call | bytes 301989888 | tf_op jit(solution)/shard_map/ring_gather/pallas_call | solution.py:186
  454.7 0.0 all-reduce.3.cloned.1.call-done
  454.7 4.6 convert_reduce_fusion.1
  459.3 1.0 fusion.8
  460.4 12.2 %fusion.30 = f32[2,416,1024]{2,1,0:T(8,128)S(1)} fusion(bf16[2,4096,1024]{2,1,0:T(8,128)(2,1)} %get-tuple-element.9, bf16[416,4096]{1,0:T(8,128)(2,1)S(1)} %get-tuple-element.24, f32[4096]{0:T(1024)S(1)} %bitcast.76, f32[4096]{0:T(1024)S(1)} %bitcast.75, f32[416]{0:T(512)S(1)} %add_rsqrt_fusion, f32[416]{0:T(512)S(1)} %broadcast_multiply_fusion), kind=kOutput, calls=%fused_computation.40 | convolution fusion | flops 6989545472 | bytes 23629056 | tf_op jit(solution)/shard_map/rk,pkn->prn/dot_general | solution.py:261
  472.6 5.2 convolution_convert_fusion.1
  477.8 0.0 reduce-scatter.5.cloned.1.call-start
  477.9 0.6 copy-done.8
  478.5 0.1 reshape.381
  478.6 0.1 copy.37
  478.7 0.1 reshape.389
  478.8 0.1 iota_compare_fusion.6
  478.9 0.1 lt.90
  479.0 0.4 convert_reduce_fusion.3
  479.4 0.1 reduce_sum.129
  479.5 0.1 mul.325
  479.5 0.1 slice_add_fusion
  479.6 0.1 eq.78
  479.8 36.9 %reduce-scatter.3.cloned.1.call-done = bf16[416,1024]{1,0:T(8,128)(2,1)} async-done(((bf16[416,4096]{1,0:T(8,128)(2,1)}), bf16[416,1024]{1,0:T(8,128)(2,1)}) %reduce-scatter.3.cloned.1.call-update) | async-done | bytes 851984 | tf_op jit(solution)/shard_map/reduce_scatter | solution.py:273
  516.7 1.7 add_convert_fusion
  518.5 2.7 gather_fusion
  521.2 1.5 convert_reduce_fusion.2
  522.7 2.6 reshape.386
  525.3 0.1 reshape.398
  525.4 0.1 reshape.400
  525.6 0.1 reduce_sum.140
  525.7 0.1 reduce_sum.141
  525.8 6.0 all-reduce
  531.8 2.8 select_convert_fusion.refs_0_
  534.7 76.1 %ring_gather.5 = bf16[896,4096]{1,0:T(8,128)(2,1)} custom-call(bf16[112,4096]{1,0:T(8,128)(2,1)} %select_convert_fusion.refs_0_), custom_call_target="tpu_custom_call" | custom-call | bytes 88080384 | tf_op jit(solution)/shard_map/ring_gather/pallas_call | solution.py:186
  610.8 6.7 %fusion.37 = bf16[1024,256]{1,0:T(8,128)(2,1)S(1)} fusion(s32[896]{0:T(1024)S(1)} %eq.78, bf16[896,4096]{1,0:T(8,128)(2,1)} %ring_gather.5, bf16[4096,256]{1,0:T(8,128)(2,1)S(1)} %bitcast.62), kind=kOutput, calls=%fused_computation.50 | convolution fusion | flops 2350219264 | bytes 9965056 | tf_op jit(solution)/shard_map/dot_general | solution.py:312
  617.5 14.7 %all_to_all.5 = bf16[8,128,256]{2,1,0:T(8,128)(2,1)S(1)} all-to-all(bf16[8,128,256]{2,1,0:T(8,128)(2,1)S(1)} %bitcast.69), channel_id=1, replica_groups=mesh['req'=8,'mlp'=4] {'req'}, dimensions={0} | all-to-all | bytes 1048576 | tf_op jit(solution)/shard_map/all_to_all | solution.py:315
  632.2 0.8 copy.45
  633.1 0.7 select_reduce_fusion
  633.8 19.3 %reduce-scatter.5.cloned.1.call-done = bf16[128,512]{1,0:T(8,128)(2,1)} async-done(((bf16[128,2048]{1,0:T(8,128)(2,1)}), bf16[128,512]{1,0:T(8,128)(2,1)}) %reduce-scatter.5.cloned.1.call-update) | async-done | bytes 131088 | tf_op jit(solution)/shard_map/reduce_scatter | solution.py:323
  653.1 1.0 multiply_reduce_fusion.1
  654.1 5.8 psum.31
  659.9 0.5 add_sqrt_fusion
  (45 shorter events, 0.3 us)
Async XLA Ops:
  7.2 603.6 %copy-start = (bf16[4,1024,256]{2,1,0:T(8,128)(2,1)S(1)}, bf16[4,1024,256]{2,1,0:T(8,128)(2,1)}, u32[]{:S(2)}) copy-start(bf16[4,1024,256]{2,1,0:T(8,128)(2,1)} %param.29) | copy-start | bytes 6291460
  188.9 2.1 copy-start.7
  188.9 2.3 copy-start.9
  200.0 2.1 copy-start.2
  206.8 2.2 copy-start.10
  212.8 241.8 %copy-start.4 = (f32[2,4096]{1,0:T(2,128)S(1)}, f32[2,4096]{1,0:T(2,128)}, u32[]{:S(2)}) copy-start(f32[2,4096]{1,0:T(2,128)} %param.22) | copy-start | bytes 98308
  214.1 240.6 %all-reduce.3.cloned.1.call-start = ((), (), s32[]{:S(2)}) async-start(), calls=%async_computation.3 | async-start | bytes 6815744 | tf_op jit(solution)/shard_map/psum | solution.py:254
  214.8 301.9 %reduce-scatter.3.cloned.1.call-start = ((), (), s32[]{:S(2)}) async-start(), calls=%async_computation.4 | async-start | bytes 4259840 | tf_op jit(solution)/shard_map/reduce_scatter | solution.py:273
  459.3 13.3 %copy-start.1 = (bf16[416,4096]{1,0:T(8,128)(2,1)}, bf16[416,4096]{1,0:T(8,128)(2,1)S(1)}, u32[]{:S(2)}) copy-start(bf16[416,4096]{1,0:T(8,128)(2,1)S(1)} %get-tuple-element.24) | copy-start | bytes 10223620
  459.3 13.3 %slice-start = ((s8[8388608]{0:T(1024)(128)(4,1)}), s8[4194304]{0:T(1024)(128)(4,1)S(1)}, s32[]{:S(2)}) async-start(s8[8388608]{0:T(1024)(128)(4,1)} %bitcast.80), calls=%async_computation.6 | async-start | bytes 8388608
  460.4 12.2 %slice-start.1 = ((s8[8388608]{0:T(1024)(128)(4,1)}), s8[4194304]{0:T(1024)(128)(4,1)S(1)}, s32[]{:S(2)}) async-start(s8[8388608]{0:T(1024)(128)(4,1)} %bitcast.80), calls=%async_computation.7 | async-start | bytes 8388608
  477.8 0.7 copy-start.8
  477.8 1.2 copy-start.3
  477.8 2.0 copy-start.5
  477.8 2.0 copy-start.6
  477.8 175.2 %reduce-scatter.5.cloned.1.call-start = ((), (), s32[]{:S(2)}) async-start(), calls=%async_computation.5 | async-start | bytes 655360 | tf_op jit(solution)/shard_map/reduce_scatter | solution.py:323
Sparse Core Ops, SparseCore 0:
  217.3 72.8 all-reduce.2
  478.0 38.7 reduce-scatter.2
  633.2 19.8 reduce-scatter.4

commit v2 on v1

--- a/solution.py
+++ b/solution.py
@@ -115,11 +115,7 @@
     return ref.at[:, pl.ds(first, count), :] if kind == "mid" else ref.at[pl.ds(first, count), :]
 
 
-def ring_kernel(n, plan, units, extra, *refs):
-    count = len(plan)
-    ins = refs[:count]
-    outs = refs[count + extra : 2 * count + extra]
-    send_sem, recv_sem, local_sem = refs[2 * count + extra :]
+def ring_steps(n, plan, units, ins, outs, send_sem, recv_sem, local_sem, work=None):
     me = lax.axis_index("req")
     place = ring_place(me, n)
     right, left = ring_device(place + 1, n), ring_device(place - 1, n)
@@ -163,12 +159,125 @@
                 )
                 keep.start()
                 local.append(keep)
+        if work is not None:
+            if step == 0:
+                local.pop(0).wait()
+                work(step, me, me)
+            else:
+                work(step, ring_device(place - step, n), ring_device(place + step, n))
     for (u, way, step), copy in started.items():
         if step == steps - 1:
             copy.wait_recv()
         copy.wait_send()
     for keep in local:
         keep.wait()
+    if work is not None:
+        last = ring_device(place + steps, n)
+        work(steps, last, last)
+
+
+def ring_kernel(n, plan, units, extra, *refs):
+    count = len(plan)
+    ring_steps(
+        n,
+        plan,
+        units,
+        refs[:count],
+        refs[count + extra : 2 * count + extra],
+        *refs[2 * count + extra :],
+    )
+
+
+def project_kernel(
+    n,
+    plan,
+    units,
+    tokens_ref,
+    gain_ref,
+    bias_ref,
+    weight_ref,
+    out_weight_ref,
+    mixed_ref,
+    out_all_ref,
+    normed,
+    gathered,
+    send_sem,
+    recv_sem,
+    local_sem,
+):
+    depth, width = weight_ref.shape
+    tile = 256
+
+    def norm_rows(block, carry):
+        rows = pl.ds(pl.multiple_of(block * 16, 16), 16)
+        normed[rows, :] = layer_norm(
+            tokens_ref[rows, :].astype(jnp.float32), gain_ref[...], bias_ref[...]
+        ).astype(jnp.bfloat16)
+        return carry
+
+    def multiply(owner, first):
+        part = pl.ds(pl.multiple_of(owner * depth, 128), depth)
+
+        def column_tile(index, carry):
+            columns = pl.ds(pl.multiple_of(index * tile, 128), tile)
+            product = jnp.dot(
+                normed[:, part], gathered[part, columns], preferred_element_type=jnp.float32
+            )
+            mixed_ref[:, columns] = product if first else mixed_ref[:, columns] + product
+            return carry
+
+        lax.fori_loop(0, width // tile, column_tile, 0)
+
+    def work(step, one, other):
+        if step == 0:
+            lax.fori_loop(0, tokens_ref.shape[0] // 16, norm_rows, 0)
+        multiply(one, step == 0)
+        if 0 < step < n // 2:
+            multiply(other, False)
+
+    ring_steps(
+        n,
+        plan,
+        units,
+        (weight_ref, out_weight_ref),
+        (gathered, out_all_ref),
+        send_sem,
+        recv_sem,
+        local_sem,
+        work,
+    )
+
+
+def norm_project(tokens, gain, bias, qkv_weight, out_weight):
+    n = lax.axis_size("req")
+    rows, model_width = tokens.shape
+    depth, width = qkv_weight.shape
+    plan = (("row", depth), ("col", out_weight.shape[1]))
+    units = ((0, 0, depth // 2), (0, depth // 2, depth // 2), (1, 0, out_weight.shape[0]))
+    anywhere, vmem = pl.BlockSpec(memory_space=pl.ANY), pl.BlockSpec(memory_space=pltpu.VMEM)
+    return pl.pallas_call(
+        functools.partial(project_kernel, n, plan, units),
+        out_shape=(
+            jax.ShapeDtypeStruct((rows, width), jnp.float32),
+            jax.ShapeDtypeStruct((out_weight.shape[0], n * out_weight.shape[1]), jnp.bfloat16),
+        ),
+        in_specs=[vmem, vmem, vmem, anywhere, anywhere],
+        out_specs=(vmem, anywhere),
+        scratch_shapes=[
+            pltpu.VMEM((rows, model_width), jnp.bfloat16),
+            pltpu.VMEM((n * depth, width), jnp.bfloat16),
+            pltpu.SemaphoreType.DMA((len(units), 2, n // 2)),
+            pltpu.SemaphoreType.DMA((len(units), 2, n // 2)),
+            pltpu.SemaphoreType.DMA((2,)),
+        ],
+        compiler_params=pltpu.CompilerParams(
+            collective_id=0, has_side_effects=True, vmem_limit_bytes=48 * 2**20
+        ),
+        cost_estimate=pl.CostEstimate(
+            flops=2 * rows * model_width * width, bytes_accessed=300 * 2**20, transcendentals=0
+        ),
+        name="norm_project",
+    )(tokens, gain, bias, qkv_weight, out_weight)
 
 
 def ring_gather(arrays, kinds, cuts, collective_id, after=()):
@@ -228,13 +337,8 @@
     slot_count = merge_rows.shape[0]
     numbers = jnp.arange(grid_sides.shape[0], dtype=jnp.int32)
     image_id, tables = row_layout(grid_sides, offsets, row_count, HEAD)
-    normed = layer_norm(tokens.astype(jnp.float32), norm_gain[0], norm_bias[0]).astype(jnp.bfloat16)
-    columns = normed
-    qkv_all, out_all = ring_gather([qkv_weight, out_weight], ["row", "col"], [2, 1], 0)
-    mixed_qkv = jnp.dot(
-        columns,
-        qkv_all,
-        preferred_element_type=jnp.float32,
+    mixed_qkv, out_all = norm_project(
+        tokens, norm_gain[:1], norm_bias[:1], qkv_weight, out_weight
     )
     heads_here = qkv_weight.shape[1] // (3 * HEAD)
     mixed_qkv = mixed_qkv.reshape(row_count, heads_here, 3, HEAD)
@@ -265,11 +369,7 @@
         preferred_element_type=jnp.float32,
     )
     hidden = (jax.nn.silu(gate_pair[0]) * gate_pair[1]).astype(jnp.bfloat16)
-    hidden_terms = jnp.dot(
-        hidden,
-        down_all,
-        preferred_element_type=jnp.float32,
-    )
+    hidden_terms = jnp.dot(hidden, down_all, preferred_element_type=jnp.float32)
     ffn_piece = lax.psum_scatter(
         hidden_terms.astype(jnp.bfloat16), "mlp", scatter_dimension=1, tiled=True
     ).astype(jnp.float32)
@@ -319,8 +419,10 @@
         concat_axis=0,
         tiled=True,
     )
-    partial = received.transpose(1, 0, 2).reshape(rows_out, groups * merge_terms.shape[1])
-    embeds = lax.psum_scatter(partial, "mlp", scatter_dimension=1, tiled=True)
+    terms = lax.all_to_all(received, "mlp", split_axis=0, concat_axis=0, tiled=True)
+    terms = terms.reshape(shards, groups // shards, rows_out, merge_terms.shape[1])
+    embeds = jnp.sum(terms.astype(jnp.float32), axis=0).astype(jnp.bfloat16)
+    embeds = embeds.transpose(1, 0, 2).reshape(rows_out, OUT // shards)
     row_squares = jnp.sum(jnp.square(embeds.astype(jnp.float32)), axis=1)
     total_squares = lax.psum(row_squares, "mlp")
     token_norms = jnp.sqrt(total_squares / OUT + EPS)

time: 668 us -> 657 us (0.984)
  matrix products: 44 us -> 32.8 us
  waiting for transfers between devices: 57 us -> 45.8 us
  local copies, waits for them, and re-layouts: 16.8 us -> 27.3 us
    pallas_call x0 -> x1, Pallas kernels: none -> 166 us  [norm_project(): pl.pallas_call(functools.partial(project_kernel, n, plan, units), out_sha...]
    pallas_call x3 -> x2, Pallas kernels: 479 us -> 316 us  [ring_gather(): pl.pallas_call(functools.partial(ring_kernel, n, tuple(plan), tuple(units...]
    reduce_scatter x1 -> x0, waiting for transfers between devices: 19.3 us -> none  [on_device(): embeds = lax.psum_scatter(partial, 'mlp', scatter_dimension=1, tiled=True)]
    dot_general x1 -> x0, matrix products: 11.2 us -> none  [on_device(): mixed_qkv = jnp.dot(columns, qkv_all, preferred_element_type=jnp.float32)]
    all_to_all x0 -> x1, waiting for transfers between devices: none -> 8.14 us  [on_device(): lax.all_to_all(received, 'mlp', split_axis=0, concat_axis=0, tiled=True)]
  transfers between devices with their start and end apart: 3 -> 3, of which waited for: 2 -> 2; matrix products, arithmetic and copies ran while one was open for 0% -> 0% of each run, Pallas kernels for 36% -> 37%
where the time goes in v2:
time: 657 us; the launch traced here: 656 us
  Pallas kernels  482 us (73%)
  waiting for transfers between devices  45.8 us (7%)
  matrix products  32.8 us (5%)
  local copies, waits for them, and re-layouts  27.3 us (4%)
  blocking collectives  27.1 us (4%)
  other arithmetic  22.9 us (3%)
  between operations  14.5 us (2%)
    pallas_call x2, Pallas kernels, ring_gather(): pl.pallas_call(functools.partial(ring_kernel, n, tuple(plan), tuple(units...  316 us
    pallas_call x1, Pallas kernels, norm_project(): pl.pallas_call(functools.partial(project_kernel, n, plan, units), out_sha...  166 us
    reduce_scatter x1, waiting for transfers between devices, on_device(): lax.psum_scatter(hidden_terms.astype(jnp.bfloat16), 'mlp', scatter_dimens...  36.9 us
    all_to_all x1, blocking collectives, on_device(): lax.all_to_all(placed_rows.reshape(groups, rows_out, merge_terms.shape[1]...  15.4 us
  transfers between devices with their start and end apart: 3, of which 2 were waited for; matrix products, arithmetic and copies ran while one was open for 0% of the time, Pallas kernels for 37%

profile of v2, /device:TPU:0, one launch (start us, length us, event | category | flops | bytes accessed | tf_op | source)
XLA Modules:
  0.0 656.3 jit_solution(15394610538933163698)
XLA Ops:
  7.2 4.3 slice.83.tokens_ref
  11.5 0.1 fusion.63
  11.6 166.5 %norm_project.1 = (f32[416,1536]{1,0:T(8,128)S(1)}, bf16[512,4096]{1,0:T(8,128)(2,1)}) custom-call(bf16[416,4096]{1,0:T(8,128)(2,1)} %slice.83.tokens_ref, f32[1,4096]{1,0:T(1,128)S(1)} %get-tuple-element.48.gain_ref, f32[1,4096]{1,0:T(1,128)S(1)} %get-tuple-element.63.bias_ref, bf16[512,1536]{1,0:T(8,128)(2,1)S(1)} %copy-done.2, bf16[512,512]{1,0:T(8,128)(2,1)S(1)} %copy-done.3), custom_call_target="tpu_custom_call" | custom-call | flops 5234491392 | bytes 314572800 | tf_op jit(solution)/shard_map/norm_project/pallas_call | solution.py:258
  178.1 1.5 copy-done.1
  179.7 3.5 copy.45
  183.1 2.8 fusion.61
  185.9 2.1 slice.109
  188.0 0.2 multiply_reduce_fusion.3
  188.3 0.1 select_reduce_fusion.4
  188.4 1.2 copy.56
  189.6 1.5 copy.57
  191.2 0.1 add_select_fusion.3
  191.3 1.5 multiply_cosine_fusion.1
  192.9 4.0 subtract_convert_fusion.3
  196.9 1.9 subtract_convert_fusion.1
  198.8 0.2 broadcast_compare_fusion
  199.0 0.3 copy.55
  199.3 3.6 fusion.14
  202.9 0.8 fusion.15
  203.7 1.3 fusion.25
  205.0 0.9 copy-done.15
  205.9 3.8 convolution_convert_fusion
  209.7 1.3 slice.120.refs_2_
  211.0 0.7 all-reduce.3.cloned.1.call-update
  211.7 0.3 reduce-scatter.2.cloned.1.call-start
  211.9 239.6 %ring_gather.2 = (bf16[2,4096,1024]{2,1,0:T(8,128)(2,1)}, bf16[1024,4096]{1,0:T(8,128)(2,1)}) custom-call(bf16[2,512,1024]{2,1,0:T(8,128)(2,1)} %refs_0_.1, bf16[1024,512]{1,0:T(8,128)(2,1)} %refs_1_.1, bf16[16,128]{1,0:T(8,128)(2,1)} %slice.120.refs_2_), custom_call_target="tpu_custom_call" | custom-call | bytes 301989888 | tf_op jit(solution)/shard_map/ring_gather/pallas_call | solution.py:295
  451.6 4.6 convert_reduce_fusion
  456.2 1.0 fusion.2
  457.3 12.2 %fusion.16 = f32[2,416,1024]{2,1,0:T(8,128)S(1)} fusion(bf16[2,4096,1024]{2,1,0:T(8,128)(2,1)} %get-tuple-element.9, bf16[416,4096]{1,0:T(8,128)(2,1)S(1)} %get-tuple-element.30, f32[4096]{0:T(1024)S(1)} %bitcast.75, f32[4096]{0:T(1024)S(1)} %bitcast.74, f32[416]{0:T(512)S(1)} %add_rsqrt_fusion, f32[416]{0:T(512)S(1)} %broadcast_multiply_fusion), kind=kOutput, calls=%fused_computation.25 | convolution fusion | flops 6989545472 | bytes 23629056 | tf_op jit(solution)/shard_map/rk,pkn->prn/dot_general | solution.py:365
  469.5 5.2 convolution_convert_fusion.1
  474.7 0.6 copy-done.13
  475.4 0.1 reshape.372
  475.4 0.1 copy.51
  475.6 0.1 reshape.381
  475.7 0.1 iota_compare_fusion.6
  475.8 0.1 lt.90
  475.9 0.4 convert_reduce_fusion.2
  476.2 0.1 reduce_sum.123
  476.3 0.1 mul.304
  476.4 0.1 slice_add_fusion
  476.5 0.1 eq.78
  476.7 36.9 %reduce-scatter.2.cloned.1.call-done = bf16[416,1024]{1,0:T(8,128)(2,1)} async-done(((bf16[416,4096]{1,0:T(8,128)(2,1)}), bf16[416,1024]{1,0:T(8,128)(2,1)}) %reduce-scatter.2.cloned.1.call-update) | async-done | bytes 851984 | tf_op jit(solution)/shard_map/reduce_scatter | solution.py:373
  513.6 1.7 add_convert_fusion.1
  515.4 2.7 gather_fusion
  518.1 1.5 convert_reduce_fusion.1
  519.6 2.6 reshape.378
  522.2 0.1 reshape.390
  522.3 0.1 reshape.392
  522.4 0.1 reduce_sum.132
  522.5 0.1 reduce_sum.133
  522.7 6.0 all-reduce
  528.7 2.8 select_convert_fusion.refs_0_
  531.5 76.1 %ring_gather.3 = bf16[896,4096]{1,0:T(8,128)(2,1)} custom-call(bf16[112,4096]{1,0:T(8,128)(2,1)} %select_convert_fusion.refs_0_), custom_call_target="tpu_custom_call" | custom-call | bytes 88080384 | tf_op jit(solution)/shard_map/ring_gather/pallas_call | solution.py:295
  607.7 6.7 %fusion.23 = bf16[1024,256]{1,0:T(8,128)(2,1)S(1)} fusion(s32[896]{0:T(1024)S(1)} %eq.78, bf16[896,4096]{1,0:T(8,128)(2,1)} %ring_gather.3, bf16[4096,256]{1,0:T(8,128)(2,1)S(1)} %bitcast.60), kind=kOutput, calls=%fused_computation.35 | convolution fusion | flops 2350219264 | bytes 9965056 | tf_op jit(solution)/shard_map/dot_general | solution.py:412
  614.4 15.4 %all_to_all.10 = bf16[8,128,256]{2,1,0:T(8,128)(2,1)} all-to-all(bf16[8,128,256]{2,1,0:T(8,128)(2,1)S(1)} %bitcast.67), channel_id=1, replica_groups=mesh['req'=8,'mlp'=4] {'req'}, dimensions={0} | all-to-all | bytes 1048576 | tf_op jit(solution)/shard_map/all_to_all | solution.py:415
  629.8 3.5 all-to-all-start.1
  633.3 0.7 select_reduce_fusion
  633.9 8.1 %all-to-all-done.1 = bf16[8,128,256]{2,1,0:T(8,128)(2,1)S(1)} async-done(((bf16[8,128,256]{2,1,0:T(8,128)(2,1)}), bf16[8,128,256]{2,1,0:T(8,128)(2,1)S(1)}, u32[]{:S(2)}, u32[]{:S(2)}) %all-to-all-start.1) | async-done | bytes 524320 | tf_op jit(solution)/shard_map/all_to_all | solution.py:422
  642.1 0.1 reduce_sum.134
  642.1 0.1 multiply_reduce_fusion.1
  642.3 0.1 copy.52
  642.4 0.8 copy.53
  643.2 5.7 psum.31
  648.9 0.5 add_sqrt_fusion
  (52 shorter events, 0.3 us)
Async XLA Ops:
  7.2 600.5 %copy-start = (bf16[4,1024,256]{2,1,0:T(8,128)(2,1)S(1)}, bf16[4,1024,256]{2,1,0:T(8,128)(2,1)}, u32[]{:S(2)}) copy-start(bf16[4,1024,256]{2,1,0:T(8,128)(2,1)} %param.29) | copy-start | bytes 6291460
  7.2 4.3 copy-start.8
  7.2 4.3 copy-start.9
  7.2 4.4 copy-start.2
  7.2 4.4 copy-start.3
  178.1 1.6 copy-start.1
  183.1 4.9 copy-start.12
  183.1 5.1 copy-start.14
  196.9 2.1 copy-start.5
  203.7 2.2 copy-start.15
  209.7 241.8 %copy-start.7 = (f32[2,4096]{1,0:T(2,128)S(1)}, f32[2,4096]{1,0:T(2,128)}, u32[]{:S(2)}) copy-start(f32[2,4096]{1,0:T(2,128)} %param.22) | copy-start | bytes 98308
  211.0 240.6 %all-reduce.3.cloned.1.call-start = ((), (), s32[]{:S(2)}) async-start(), calls=%async_computation.3 | async-start | bytes 6815744 | tf_op jit(solution)/shard_map/psum | solution.py:358
  211.7 301.9 %reduce-scatter.2.cloned.1.call-start = ((), (), s32[]{:S(2)}) async-start(), calls=%async_computation.4 | async-start | bytes 4259840 | tf_op jit(solution)/shard_map/reduce_scatter | solution.py:373
  456.2 13.3 %copy-start.4 = (bf16[416,4096]{1,0:T(8,128)(2,1)}, bf16[416,4096]{1,0:T(8,128)(2,1)S(1)}, u32[]{:S(2)}) copy-start(bf16[416,4096]{1,0:T(8,128)(2,1)S(1)} %get-tuple-element.30) | copy-start | bytes 10223620
  456.2 13.3 %slice-start = ((s8[8388608]{0:T(1024)(128)(4,1)}), s8[4194304]{0:T(1024)(128)(4,1)S(1)}, s32[]{:S(2)}) async-start(s8[8388608]{0:T(1024)(128)(4,1)} %bitcast.77), calls=%async_computation.5 | async-start | bytes 8388608
  457.3 12.2 %slice-start.1 = ((s8[8388608]{0:T(1024)(128)(4,1)}), s8[4194304]{0:T(1024)(128)(4,1)S(1)}, s32[]{:S(2)}) async-start(s8[8388608]{0:T(1024)(128)(4,1)} %bitcast.77), calls=%async_computation.6 | async-start | bytes 8388608
  474.7 0.7 copy-start.13
  474.7 1.2 copy-start.6
  474.7 2.0 copy-start.10
  474.7 2.0 copy-start.11
  629.8 12.3 %all-to-all-start.1 = ((bf16[8,128,256]{2,1,0:T(8,128)(2,1)}), bf16[8,128,256]{2,1,0:T(8,128)(2,1)S(1)}, u32[]{:S(2)}, u32[]{:S(2)}) async-start(bf16[8,128,256]{2,1,0:T(8,128)(2,1)} %all_to_all.10), calls=%async_computation.2 | async-start | bytes 1048576 | tf_op jit(solution)/shard_map/all_to_all | solution.py:422
Sparse Core Ops, SparseCore 0:
  214.1 72.8 all-reduce.2
  474.8 38.7 reduce-scatter.1

commit v3 on v2

--- a/solution.py
+++ b/solution.py
@@ -58,27 +58,9 @@
     return (image_id, (jnp.cos(angle_y), jnp.sin(angle_y), jnp.cos(angle_x), jnp.sin(angle_x)))
 
 
-def rotate(vectors, tables):
-    cos_y, sin_y, cos_x, sin_x = tables
-    quarter = vectors.shape[-1] // 4
-    upper_y = vectors[..., :quarter]
-    lower_y = vectors[..., quarter : 2 * quarter]
-    upper_x = vectors[..., 2 * quarter : 3 * quarter]
-    lower_x = vectors[..., 3 * quarter :]
-    return jnp.concatenate(
-        [
-            upper_y * cos_y - lower_y * sin_y,
-            upper_y * sin_y + lower_y * cos_y,
-            upper_x * cos_x - lower_x * sin_x,
-            upper_x * sin_x + lower_x * cos_x,
-        ],
-        axis=-1,
-    )
-
-
 def attend(queries, key_rows, values, image_id, numbers):
     scores = jnp.einsum(
-        "qhd,khd->hqk", queries, key_rows, preferred_element_type=jnp.float32
+        "hqd,hkd->hqk", queries, key_rows, preferred_element_type=jnp.float32
     ) / math.sqrt(queries.shape[-1])
     same_image = image_id[:, None] == image_id[None, :]
     scores = jnp.where(same_image[None], scores, -jnp.inf)
@@ -86,7 +68,7 @@
     expo_vals = jnp.exp(scores - row_peak[..., None])
     weights = (expo_vals / jnp.sum(expo_vals, axis=-1, keepdims=True)).astype(jnp.bfloat16)
     attended = jnp.einsum(
-        "hqk,khd->qhd", weights, values, preferred_element_type=jnp.float32
+        "hqk,hkd->qhd", weights, values, preferred_element_type=jnp.float32
     ).astype(jnp.bfloat16)
     owned = image_id[None, None, :] == numbers[:, None, None]
     logits = jnp.max(jnp.where(owned, row_peak[None], -jnp.inf), axis=-1)
@@ -197,13 +179,20 @@
     bias_ref,
     weight_ref,
     out_weight_ref,
+    cos_ref,
+    sin_ref,
+    queries_ref,
+    keys_ref,
+    values_ref,
+    out_all_ref,
+    tokens_in,
     mixed_ref,
-    out_all_ref,
     normed,
     gathered,
     send_sem,
     recv_sem,
     local_sem,
+    tokens_sem,
 ):
     depth, width = weight_ref.shape
     tile = 256
@@ -211,7 +200,7 @@
     def norm_rows(block, carry):
         rows = pl.ds(pl.multiple_of(block * 16, 16), 16)
         normed[rows, :] = layer_norm(
-            tokens_ref[rows, :].astype(jnp.float32), gain_ref[...], bias_ref[...]
+            tokens_in[rows, :].astype(jnp.float32), gain_ref[...], bias_ref[...]
         ).astype(jnp.bfloat16)
         return carry
 
@@ -230,11 +219,16 @@
 
     def work(step, one, other):
         if step == 0:
-            lax.fori_loop(0, tokens_ref.shape[0] // 16, norm_rows, 0)
+            fetch.wait()
+            lax.fori_loop(0, tokens_in.shape[0] // 16, norm_rows, 0)
         multiply(one, step == 0)
         if 0 < step < n // 2:
             multiply(other, False)
 
+    fetch = pltpu.make_async_copy(
+        tokens_ref.at[pl.ds(0, tokens_in.shape[0]), :], tokens_in, tokens_sem.at[0]
+    )
+    fetch.start()
     ring_steps(
         n,
         plan,
@@ -246,29 +240,50 @@
         local_sem,
         work,
     )
-
-
-def norm_project(tokens, gain, bias, qkv_weight, out_weight):
+    lane = lax.broadcasted_iota(jnp.int32, (1, HEAD), 1)
+    leading = lane // (HEAD // 4) % 2 == 0
+    for head in range(width // (3 * HEAD)):
+        for j, target in enumerate((queries_ref, keys_ref)):
+            vectors = mixed_ref[:, (3 * head + j) * HEAD : (3 * head + j + 1) * HEAD]
+            partner = jnp.where(
+                leading,
+                pltpu.roll(vectors, HEAD - HEAD // 4, 1),
+                pltpu.roll(vectors, HEAD // 4, 1),
+            )
+            target[head] = (vectors * cos_ref[...] + partner * sin_ref[...]).astype(jnp.bfloat16)
+        values_ref[head] = mixed_ref[:, (3 * head + 2) * HEAD : (3 * head + 3) * HEAD].astype(
+            jnp.bfloat16
+        )
+
+
+def norm_project(tokens, rows, gain, bias, qkv_weight, out_weight, cosines, sines):
     n = lax.axis_size("req")
-    rows, model_width = tokens.shape
+    model_width = tokens.shape[1]
     depth, width = qkv_weight.shape
     plan = (("row", depth), ("col", out_weight.shape[1]))
     units = ((0, 0, depth // 2), (0, depth // 2, depth // 2), (1, 0, out_weight.shape[0]))
+    heads = width // (3 * HEAD)
+    by_head = jax.ShapeDtypeStruct((heads, rows, HEAD), jnp.bfloat16)
     anywhere, vmem = pl.BlockSpec(memory_space=pl.ANY), pl.BlockSpec(memory_space=pltpu.VMEM)
     return pl.pallas_call(
         functools.partial(project_kernel, n, plan, units),
         out_shape=(
-            jax.ShapeDtypeStruct((rows, width), jnp.float32),
+            by_head,
+            by_head,
+            by_head,
             jax.ShapeDtypeStruct((out_weight.shape[0], n * out_weight.shape[1]), jnp.bfloat16),
         ),
-        in_specs=[vmem, vmem, vmem, anywhere, anywhere],
-        out_specs=(vmem, anywhere),
+        in_specs=[anywhere, vmem, vmem, anywhere, anywhere, vmem, vmem],
+        out_specs=(vmem, vmem, vmem, anywhere),
         scratch_shapes=[
+            pltpu.VMEM((rows, model_width), jnp.bfloat16),
+            pltpu.VMEM((rows, width), jnp.float32),
             pltpu.VMEM((rows, model_width), jnp.bfloat16),
             pltpu.VMEM((n * depth, width), jnp.bfloat16),
             pltpu.SemaphoreType.DMA((len(units), 2, n // 2)),
             pltpu.SemaphoreType.DMA((len(units), 2, n // 2)),
             pltpu.SemaphoreType.DMA((2,)),
+            pltpu.SemaphoreType.DMA((1,)),
         ],
         compiler_params=pltpu.CompilerParams(
             collective_id=0, has_side_effects=True, vmem_limit_bytes=48 * 2**20
@@ -277,7 +292,7 @@
             flops=2 * rows * model_width * width, bytes_accessed=300 * 2**20, transcendentals=0
         ),
         name="norm_project",
-    )(tokens, gain, bias, qkv_weight, out_weight)
+    )(tokens, gain, bias, qkv_weight, out_weight, cosines, sines)
 
 
 def ring_gather(arrays, kinds, cuts, collective_id, after=()):
@@ -327,7 +342,7 @@
 ):
     images = grid_sides.shape[0]
     row_count = min(tokens.shape[0], -(-images * (5 + GMAX * GMAX) // 16) * 16)
-    tokens = tokens[:row_count]
+    all_tokens, tokens = tokens, tokens[:row_count]
     model_width = tokens.shape[1]
     groups = lax.axis_size("req")
     shards = lax.axis_size("mlp")
@@ -337,14 +352,18 @@
     slot_count = merge_rows.shape[0]
     numbers = jnp.arange(grid_sides.shape[0], dtype=jnp.int32)
     image_id, tables = row_layout(grid_sides, offsets, row_count, HEAD)
-    mixed_qkv, out_all = norm_project(
-        tokens, norm_gain[:1], norm_bias[:1], qkv_weight, out_weight
-    )
+    cos_y, sin_y, cos_x, sin_x = (table[:, 0] for table in tables)
     heads_here = qkv_weight.shape[1] // (3 * HEAD)
-    mixed_qkv = mixed_qkv.reshape(row_count, heads_here, 3, HEAD)
-    queries = rotate(mixed_qkv[:, :, 0], tables).astype(jnp.bfloat16)
-    key_rows = rotate(mixed_qkv[:, :, 1], tables).astype(jnp.bfloat16)
-    values = mixed_qkv[:, :, 2].astype(jnp.bfloat16)
+    queries, key_rows, values, out_all = norm_project(
+        all_tokens,
+        row_count,
+        norm_gain[:1],
+        norm_bias[:1],
+        qkv_weight,
+        out_weight,
+        jnp.concatenate([cos_y, cos_y, cos_x, cos_x], axis=1),
+        jnp.concatenate([-sin_y, sin_y, -sin_x, sin_x], axis=1),
+    )
     attended, logits = attend(queries, key_rows, values, image_id, numbers)
     attended_flat = attended.reshape(row_count, heads_here * HEAD)
     head_terms = jnp.dot(

time: 657 us -> 633 us (0.963)
  local copies, waits for them, and re-layouts: 27.3 us -> 10.8 us
    slice x3 -> x0, local copies, waits for them, and re-layouts: 9.2 us -> none  [the longest x1 4.28 us: on_device(): tokens = tokens[:row_count]]
  transfers between devices with their start and end apart: 3 -> 3, of which waited for: 2 -> 2; matrix products, arithmetic and copies ran while one was open for 0% -> 0% of each run, Pallas kernels for 37% -> 38%
where the time goes in v3:
time: 633 us
  Pallas kernels  481 us (76%)
  waiting for transfers between devices  45.8 us (7%)
  matrix products  29.9 us (5%)
  blocking collectives  27.1 us (4%)
  other arithmetic  19.6 us (3%)
  between operations  14.4 us (2%)
  local copies, waits for them, and re-layouts  10.8 us (2%)
    pallas_call x2, Pallas kernels, ring_gather(): pl.pallas_call(functools.partial(ring_kernel, n, tuple(plan), tuple(units...  316 us
    pallas_call x1, Pallas kernels, norm_project(): pl.pallas_call(functools.partial(project_kernel, n, plan, units), out_sha...  166 us
    reduce_scatter x1, waiting for transfers between devices, on_device(): lax.psum_scatter(hidden_terms.astype(jnp.bfloat16), 'mlp', scatter_dimens...  36.9 us
    all_to_all x1, blocking collectives, on_device(): lax.all_to_all(placed_rows.reshape(groups, rows_out, merge_terms.shape[1]...  15.4 us
  transfers between devices with their start and end apart: 3, of which 2 were waited for; matrix products, arithmetic and copies ran while one was open for 0% of the time, Pallas kernels for 38%

profile of v3, /device:TPU:0, one launch (start us, length us, event | category | flops | bytes accessed | tf_op | source)
XLA Modules:
  0.0 632.5 jit_solution(11785698908781089014)
XLA Ops:
  7.2 0.0 copy-start
  7.2 0.0 copy-start.1
  7.2 1.1 multiply_reduce_fusion.3
  8.3 0.7 add_add_fusion.1
  9.0 0.8 select_reduce_fusion.1
  9.8 0.2 broadcast_compare_fusion
  10.0 0.9 fusion.46
  10.9 0.1 add_select_fusion.3
  11.0 1.6 fusion.30
  12.6 0.4 pad_maximum_fusion
  13.0 165.6 %norm_project.1 = (bf16[4,416,128]{2,1,0:T(8,128)(2,1)S(1)}, bf16[4,416,128]{2,1,0:T(8,128)(2,1)S(1)}, bf16[4,416,128]{2,1,0:T(8,128)(2,1)S(1)}, bf16[512,4096]{1,0:T(8,128)(2,1)}) custom-call(bf16[512,4096]{1,0:T(8,128)(2,1)} %tokens_ref.1, f32[1,4096]{1,0:T(1,128)S(1)} %get-tuple-element.41.gain_ref, f32[1,4096]{1,0:T(1,128)S(1)} %get-tuple-element.61.bias_ref, ...), custom_call_target="tpu_custom_call" | custom-call | flops 5234491392 | bytes 314572800 | tf_op jit(solution)/shard_map/norm_project/pallas_call | solution.py:268
  178.6 0.8 fusion.14
  179.4 0.8 fusion.15
  180.2 0.0 copy-start.9
  180.2 1.3 fusion.25
  181.5 0.9 copy-done.9
  182.4 3.8 convolution_convert_fusion
  186.1 1.3 slice.64.refs_2_
  187.4 0.7 all-reduce.3.cloned.1.call-update
  188.1 0.2 reduce-scatter.2.cloned.1.call-start
  188.4 239.6 %ring_gather.2 = (bf16[2,4096,1024]{2,1,0:T(8,128)(2,1)}, bf16[1024,4096]{1,0:T(8,128)(2,1)}) custom-call(bf16[2,512,1024]{2,1,0:T(8,128)(2,1)} %refs_0_.1, bf16[1024,512]{1,0:T(8,128)(2,1)} %refs_1_.1, bf16[16,128]{1,0:T(8,128)(2,1)} %slice.64.refs_2_), custom_call_target="tpu_custom_call" | custom-call | bytes 301989888 | tf_op jit(solution)/shard_map/ring_gather/pallas_call | solution.py:310
  428.0 0.0 all-reduce.3.cloned.1.call-done
  428.0 4.6 convert_reduce_fusion
  432.6 0.0 slice-start
  432.7 1.0 fusion.2
  433.7 0.0 slice-start.1
  433.7 12.2 %fusion.16 = f32[2,416,1024]{2,1,0:T(8,128)S(1)} fusion(bf16[2,4096,1024]{2,1,0:T(8,128)(2,1)} %get-tuple-element.13, bf16[416,4096]{1,0:T(8,128)(2,1)S(1)} %get-tuple-element.37, f32[4096]{0:T(1024)S(1)} %bitcast.68, f32[4096]{0:T(1024)S(1)} %bitcast.67, f32[416]{0:T(512)S(1)} %add_rsqrt_fusion, f32[416]{0:T(512)S(1)} %broadcast_multiply_fusion), kind=kOutput, calls=%fused_computation.25 | convolution fusion | flops 6989545472 | bytes 23629056 | tf_op jit(solution)/shard_map/rk,pkn->prn/dot_general | solution.py:384
  445.9 5.2 convolution_convert_fusion.1
  451.1 0.0 reduce-scatter.2.cloned.1.call-update
  451.1 0.6 copy-done.8
  451.8 0.1 reshape.321
  451.8 0.1 copy.39
  452.0 0.1 reshape.330
  452.1 0.1 iota_compare_fusion.6
  452.1 0.1 lt.90
  452.3 0.0 copy-done.4
  452.3 0.4 convert_reduce_fusion.2
  452.6 0.1 reduce_sum.123
  452.7 0.1 mul.194
  452.8 0.1 slice_add_fusion
  452.9 0.1 eq.78
  453.1 36.9 %reduce-scatter.2.cloned.1.call-done = bf16[416,1024]{1,0:T(8,128)(2,1)} async-done(((bf16[416,4096]{1,0:T(8,128)(2,1)}), bf16[416,1024]{1,0:T(8,128)(2,1)}) %reduce-scatter.2.cloned.1.call-update) | async-done | bytes 851984 | tf_op jit(solution)/shard_map/reduce_scatter | solution.py:392
  490.0 1.7 add_convert_fusion.1
  491.7 2.7 gather_fusion
  494.5 1.5 convert_reduce_fusion.1
  496.0 2.6 reshape.327
  498.6 0.1 reshape.339
  498.7 0.1 reshape.341
  498.8 0.1 reduce_sum.132
  498.9 0.1 reduce_sum.133
  499.0 6.0 all-reduce
  505.0 2.8 select_convert_fusion.refs_0_
  507.9 76.1 %ring_gather.3 = bf16[896,4096]{1,0:T(8,128)(2,1)} custom-call(bf16[112,4096]{1,0:T(8,128)(2,1)} %select_convert_fusion.refs_0_), custom_call_target="tpu_custom_call" | custom-call | bytes 88080384 | tf_op jit(solution)/shard_map/ring_gather/pallas_call | solution.py:310
  584.0 6.7 %fusion.23 = bf16[1024,256]{1,0:T(8,128)(2,1)S(1)} fusion(s32[896]{0:T(1024)S(1)} %eq.78, bf16[896,4096]{1,0:T(8,128)(2,1)} %ring_gather.3, bf16[4096,256]{1,0:T(8,128)(2,1)S(1)} %bitcast.57), kind=kOutput, calls=%fused_computation.35 | convolution fusion | flops 2350219264 | bytes 9965056 | tf_op jit(solution)/shard_map/dot_general | solution.py:431
  590.7 15.4 %all_to_all.10 = bf16[8,128,256]{2,1,0:T(8,128)(2,1)} all-to-all(bf16[8,128,256]{2,1,0:T(8,128)(2,1)S(1)} %bitcast.60), channel_id=1, replica_groups=mesh['req'=8,'mlp'=4] {'req'}, dimensions={0} | all-to-all | bytes 1048576 | tf_op jit(solution)/shard_map/all_to_all | solution.py:434
  606.1 3.5 all-to-all-start.1
  609.6 0.7 select_reduce_fusion
  610.2 8.1 %all-to-all-done.1 = bf16[8,128,256]{2,1,0:T(8,128)(2,1)S(1)} async-done(((bf16[8,128,256]{2,1,0:T(8,128)(2,1)}), bf16[8,128,256]{2,1,0:T(8,128)(2,1)S(1)}, u32[]{:S(2)}, u32[]{:S(2)}) %all-to-all-start.1) | async-done | bytes 524320 | tf_op jit(solution)/shard_map/all_to_all | solution.py:441
  618.4 0.1 reduce_sum.134
  618.4 0.1 multiply_reduce_fusion.1
  618.5 0.1 copy.40
  618.7 0.8 copy.41
  619.5 5.7 psum.31
  625.2 0.5 add_sqrt_fusion
  (32 shorter events, 0.2 us)
Async XLA Ops:
  7.2 576.8 %copy-start = (bf16[4,1024,256]{2,1,0:T(8,128)(2,1)S(1)}, bf16[4,1024,256]{2,1,0:T(8,128)(2,1)}, u32[]{:S(2)}) copy-start(bf16[4,1024,256]{2,1,0:T(8,128)(2,1)} %param.29) | copy-start | bytes 6291460
  7.2 5.8 copy-start.1
  7.2 5.8 copy-start.2
  180.2 2.2 copy-start.9
  186.1 241.8 %copy-start.5 = (f32[2,4096]{1,0:T(2,128)S(1)}, f32[2,4096]{1,0:T(2,128)}, u32[]{:S(2)}) copy-start(f32[2,4096]{1,0:T(2,128)} %param.22) | copy-start | bytes 98308
  187.4 240.6 %all-reduce.3.cloned.1.call-start = ((), (), s32[]{:S(2)}) async-start(), calls=%async_computation.3 | async-start | bytes 6815744 | tf_op jit(solution)/shard_map/psum | solution.py:377
  188.1 301.9 %reduce-scatter.2.cloned.1.call-start = ((), (), s32[]{:S(2)}) async-start(), calls=%async_computation.4 | async-start | bytes 4259840 | tf_op jit(solution)/shard_map/reduce_scatter | solution.py:392
  432.6 13.2 %copy-start.3 = (bf16[416,4096]{1,0:T(8,128)(2,1)}, bf16[416,4096]{1,0:T(8,128)(2,1)S(1)}, u32[]{:S(2)}) copy-start(bf16[416,4096]{1,0:T(8,128)(2,1)S(1)} %get-tuple-element.37) | copy-start | bytes 10223620
  432.6 13.2 %slice-start = ((s8[8388608]{0:T(1024)(128)(4,1)}), s8[4194304]{0:T(1024)(128)(4,1)S(1)}, s32[]{:S(2)}) async-start(s8[8388608]{0:T(1024)(128)(4,1)} %bitcast.70), calls=%async_computation.5 | async-start | bytes 8388608
  433.7 12.2 %slice-start.1 = ((s8[8388608]{0:T(1024)(128)(4,1)}), s8[4194304]{0:T(1024)(128)(4,1)S(1)}, s32[]{:S(2)}) async-start(s8[8388608]{0:T(1024)(128)(4,1)} %bitcast.70), calls=%async_computation.6 | async-start | bytes 8388608
  451.1 0.7 copy-start.8
  451.1 1.2 copy-start.4
  451.1 2.0 copy-start.6
  451.1 2.0 copy-start.7
  606.1 12.3 %all-to-all-start.1 = ((bf16[8,128,256]{2,1,0:T(8,128)(2,1)}), bf16[8,128,256]{2,1,0:T(8,128)(2,1)S(1)}, u32[]{:S(2)}, u32[]{:S(2)}) async-start(bf16[8,128,256]{2,1,0:T(8,128)(2,1)} %all_to_all.10), calls=%async_computation.2 | async-start | bytes 1048576 | tf_op jit(solution)/shard_map/all_to_all | solution.py:441
Sparse Core Ops, SparseCore 0:
  190.6 72.8 all-reduce.2
  451.2 38.7 reduce-scatter.1
